TPU v7x, 128 devices: a whole 4x4x4 slice. The times are simulated.
128 devices in a mesh: pair: 64 (over x, z_hi, y, core), ga: 2 (over z_lo).
Axes of the slice: x: 4, y: 4, z: 4 (z_hi: 2, z_lo: 2; z = z_hi * 2 + z_lo), core: 2. Of those that a mesh axis runs over, the one named last changes fastest.
Arguments:
- pair_valence: bfloat16 [64, 16384], P(None, 'ga'), may hold values from -6 to 6
- screened: bfloat16 [16384, 16384], P('ga', 'pair'), may hold values from -0.046875 to 0.046875
- pair_conduction: bfloat16 [65536, 16384], P(('pair', 'ga')), may hold values from -0.4375 to 0.4375
- pair_mixed: bfloat16 [8192, 16384], P('ga', 'pair'), may hold values from -3.5 to 3.5
- coulomb: float32 [16384], P('pair'), may hold values from 0.2 to 5
Outputs:
- direct: float32 [65536, 64], P(('pair', 'ga'))
- exchange: float32 [8192, 512], P(('ga', 'pair'))
All inputs are finite; a program needn't handle non-finite values.
Results may differ from a plain program's by a relative error of at most 0.0029.
Values may be sent and summed in bfloat16 or wider, within the bound.
A program may use at most 192 MiB of HBM per device.

v0:
```python
import jax
import jax.numpy as jnp
from jax import lax
from jax.sharding import PartitionSpec as P

NC = 256
V_WIN = 2


def spread(value, axis, source):
    kept = jnp.where(lax.axis_index(axis) == source, value, 0).astype(value.dtype)
    return lax.psum(kept, axis)


def local(pair_valence, screened, pair_conduction, pair_mixed, coulomb):
    slab = jnp.dot(pair_valence, screened, preferred_element_type=jnp.float32)
    images = lax.psum(slab, "ga").astype(jnp.bfloat16)
    swapped = lax.all_to_all(pair_conduction, "pair", split_axis=1, concat_axis=0, tiled=True)
    picked = swapped
    direct = lax.psum_scatter(
        jnp.einsum("ck,vk->cv", picked, images, preferred_element_type=jnp.float32),
        "pair",
        scatter_dimension=0,
        tiled=True,
    )
    window_count = V_WIN * NC
    window_top = pair_mixed[:window_count]
    window = spread(window_top, "ga", 0)
    scaled = (window.astype(jnp.float32) * coulomb).astype(jnp.bfloat16)
    picked = pair_mixed
    exchange = lax.psum_scatter(
        jnp.einsum("gk,xk->gx", picked, scaled, preferred_element_type=jnp.float32),
        "pair",
        scatter_dimension=0,
        tiled=True,
    )
    return (direct, exchange)


def solution(mesh):
    return jax.shard_map(
        local,
        mesh=mesh,
        in_specs=(
            P(None, "ga"),
            P("ga", "pair"),
            P(("pair", "ga"), None),
            P("ga", "pair"),
            P("pair"),
        ),
        out_specs=(P(("pair", "ga"), None), P(("ga", "pair"), None)),
        check_vma=False,
    )
```

profile of v0, /device:TPU:32, one launch (start us, length us, event | category | flops | bytes accessed | tf_op | source)
XLA Modules:
  0.0 954.2 jit_solution(1627960435851854184)
XLA Ops:
  7.2 0.0 copy-start
  7.2 22.5 %copy.12 = bf16[512,16384]{0,1:T(8,128)(2,1)} copy(bf16[512,16384]{1,0:T(8,128)(2,1)} %param.7) | data formatting | bytes 33554432 | tf_op args[2]
  29.7 10.7 %all-to-all-start = ((bf16[512,64,256]{0,2,1:T(8,128)(2,1)}), bf16[512,64,256]{0,2,1:T(8,128)(2,1)}, u32[]{:S(2)}, u32[]{:S(2)}) async-start(bf16[512,64,256]{0,2,1:T(8,128)(2,1)} %bitcast.14), calls=%async_computation | async-start | bytes 33554432 | tf_op jit(solution)/shard_map/all_to_all | solution.py:18
  40.4 0.0 all-reduce.2.cloned.1.call-start
  40.5 0.0 copy-done.2
  40.5 0.7 slice_select_fusion
  41.2 0.0 all-reduce.2.cloned.1.call-update
  41.2 0.0 reduce-scatter.7.cloned.1.call-start
  41.3 158.5 %all-reduce.2.cloned.1.call-done = bf16[512,256]{1,0:T(8,128)(2,1)} async-done(((bf16[512,256]{1,0:T(8,128)(2,1)}), bf16[512,256]{1,0:T(8,128)(2,1)}) %all-reduce.2.cloned.1.call-update) | async-done | bytes 262160 | tf_op jit(solution)/shard_map/psum | solution.py:12
  199.8 0.0 copy-done.3
  199.8 5.4 convolution_bitcast_fusion.1
  205.3 9.0 copy.15
  214.3 0.0 reduce-scatter.7.cloned.1.call-update
  214.3 0.0 reduce-scatter.5.cloned.1.call-start
  214.4 0.0 copy-done
  214.4 3.0 fusion.2
  217.4 27.1 %psum.14 = bf16[64,256]{1,0:T(8,128)(2,1)S(1)} all-reduce(f32[64,256]{1,0:T(8,128)S(1)} %fusion.2), channel_id=1, replica_groups=mesh['pair'=64,'ga'=2] {'ga'}, use_global_device_ids=true, to_apply=%region_0.0 | all-reduce | flops 16384 | bytes 98304 | tf_op jit(solution)/shard_map/psum | solution.py:17
  244.5 19.7 %all-to-all-done = bf16[512,64,256]{0,2,1:T(8,128)(2,1)} async-done(((bf16[512,64,256]{0,2,1:T(8,128)(2,1)}), bf16[512,64,256]{0,2,1:T(8,128)(2,1)}, u32[]{:S(2)}, u32[]{:S(2)}) %all-to-all-start) | async-done | bytes 16777248 | tf_op jit(solution)/shard_map/all_to_all | solution.py:18
  264.2 22.3 %copy.13 = bf16[64,512,256]{2,1,0:T(8,128)(2,1)} copy(bf16[64,512,256]{1,2,0:T(8,128)(2,1)} %bitcast.1) | data formatting | bytes 33554432 | tf_op jit(solution)/shard_map/all_to_all | solution.py:18
  286.5 14.3 %convolution_bitcast_fusion = f32[32768,64]{0,1:T(8,128)} fusion(bf16[32768,256]{1,0:T(8,128)(2,1)} %bitcast.13, bf16[64,256]{1,0:T(8,128)(2,1)S(1)} %psum.14), kind=kOutput, calls=%fused_computation | convolution fusion | flops 1073741824 | bytes 25198592 | tf_op jit(solution)/shard_map/ck,vk->cv/dot_general | solution.py:21
  300.7 0.0 reduce-scatter.5.cloned.1.call-update
  300.8 303.2 %reduce-scatter.7.cloned.1.call-done = f32[64,512]{1,0:T(8,128)} async-done(((f32[4096,512]{1,0:T(8,128)}), f32[64,512]{1,0:T(8,128)}) %reduce-scatter.7.cloned.1.call-update) | async-done | bytes 131088
  603.9 343.7 %reduce-scatter.5.cloned.1.call-done = f32[512,64]{0,1:T(8,128)} async-done(((f32[32768,64]{0,1:T(8,128)}), f32[512,64]{0,1:T(8,128)}) %reduce-scatter.5.cloned.1.call-update) | async-done | bytes 131088 | tf_op jit(solution)/shard_map/reduce_scatter | solution.py:20
  947.6 0.0 copy-done.1
  (3 shorter events, 0.0 us)
Async XLA Ops:
  7.2 207.2 %copy-start = (bf16[64,8192]{1,0:T(8,128)(2,1)S(1)}, bf16[64,8192]{1,0:T(8,128)(2,1)}, u32[]{:S(2)}) copy-start(bf16[64,8192]{1,0:T(8,128)(2,1)} %param.5) | copy-start | bytes 3145732
  29.7 10.8 %copy-start.2 = (bf16[4096,256]{1,0:T(8,128)(2,1)S(1)}, bf16[4096,256]{1,0:T(8,128)(2,1)}, u32[]{:S(2)}) copy-start(bf16[4096,256]{1,0:T(8,128)(2,1)} %param.8) | copy-start | bytes 6291460
  29.7 170.2 %copy-start.3 = (f32[256]{0:T(256)S(1)}, f32[256]{0:T(256)}, u32[]{:S(2)}) copy-start(f32[256]{0:T(256)} %param.9) | copy-start | bytes 3076
  29.7 234.5 %all-to-all-start = ((bf16[512,64,256]{0,2,1:T(8,128)(2,1)}), bf16[512,64,256]{0,2,1:T(8,128)(2,1)}, u32[]{:S(2)}, u32[]{:S(2)}) async-start(bf16[512,64,256]{0,2,1:T(8,128)(2,1)} %bitcast.14), calls=%async_computation | async-start | bytes 33554432 | tf_op jit(solution)/shard_map/all_to_all | solution.py:18
  40.4 159.4 %all-reduce.2.cloned.1.call-start = ((), (), s32[]{:S(2)}) async-start(), calls=%async_computation.4 | async-start | bytes 524288 | tf_op jit(solution)/shard_map/psum | solution.py:12
  41.2 562.7 %reduce-scatter.7.cloned.1.call-start = ((), (), s32[]{:S(2)}) async-start(), calls=%async_computation.5 | async-start | bytes 8519680
  214.3 733.3 %reduce-scatter.5.cloned.1.call-start = ((), (), s32[]{:S(2)}) async-start(), calls=%async_computation.3 | async-start | bytes 8519680 | tf_op jit(solution)/shard_map/reduce_scatter | solution.py:20
  286.4 661.2 %copy-start.1 = (bf16[64,8192]{1,0:T(8,128)(2,1)S(1)}, bf16[64,8192]{1,0:T(8,128)(2,1)}, u32[]{:S(2)}) copy-start(bf16[64,8192]{1,0:T(8,128)(2,1)} %param.5) | copy-start | bytes 3145732
Sparse Core Ops, SparseCore 0:
  43.7 156.0 all-reduce.1
  214.5 389.4 reduce-scatter.6
  607.0 340.5 reduce-scatter.4
where the time goes:
time: 957 us; the launch traced here: 954 us
  waiting for transfers between devices  825 us (86%)
  local copies, waits for them, and re-layouts  53.9 us (6%)
  blocking collectives  27.1 us (3%)
  matrix products  22.7 us (2%)
  between operations  13.8 us (1%)
  starting transfers between devices  10.9 us (1%)
    reduce_scatter x1, waiting for transfers between devices, local(): lax.psum_scatter(jnp.einsum('ck,vk->cv', picked, images, preferred_elemen...  344 us
    unnamed x4, waiting for transfers between devices  303 us
    psum x1, waiting for transfers between devices, spread(): return lax.psum(kept, axis)  159 us
    unnamed x10, local copies, waits for them, and re-layouts  31.6 us
    psum x1, blocking collectives, local(): images = lax.psum(slab, 'ga').astype(jnp.bfloat16)  27.1 us
    all_to_all x1, local copies, waits for them, and re-layouts, local(): lax.all_to_all(pair_conduction, 'pair', split_axis=1, concat_axis=0, tile...  22.3 us
    all_to_all x1, waiting for transfers between devices, local(): lax.all_to_all(pair_conduction, 'pair', split_axis=1, concat_axis=0, tile...  19.7 us
  transfers between devices with their start and end apart: 4, of which 4 were waited for; matrix products, arithmetic and copies ran while one was open for 6% of the time, Pallas kernels for 0%

commit v1 on v0

--- a/solution.py
+++ b/solution.py
@@ -15,14 +15,8 @@
 def local(pair_valence, screened, pair_conduction, pair_mixed, coulomb):
     slab = jnp.dot(pair_valence, screened, preferred_element_type=jnp.float32)
     images = lax.psum(slab, "ga").astype(jnp.bfloat16)
-    swapped = lax.all_to_all(pair_conduction, "pair", split_axis=1, concat_axis=0, tiled=True)
-    picked = swapped
-    direct = lax.psum_scatter(
-        jnp.einsum("ck,vk->cv", picked, images, preferred_element_type=jnp.float32),
-        "pair",
-        scatter_dimension=0,
-        tiled=True,
-    )
+    images = lax.all_gather(images, "pair", axis=1, tiled=True)
+    direct = jnp.einsum("ck,vk->cv", pair_conduction, images, preferred_element_type=jnp.float32)
     window_count = V_WIN * NC
     window_top = pair_mixed[:window_count]
     window = spread(window_top, "ga", 0)

time: 957 us -> 449 us (0.47)
  waiting for transfers between devices: 825 us -> 392 us
  local copies, waits for them, and re-layouts: 53.9 us -> 9.05 us
  blocking collectives: 27.1 us -> 7.96 us
  starting transfers between devices: 10.9 us -> 0.13 us
    reduce_scatter x1 -> x0, waiting for transfers between devices: 344 us -> none  [local(): lax.psum_scatter(jnp.einsum('ck,vk->cv', picked, images, preferred_elemen...]
    psum x1, waiting for transfers between devices: 159 us -> 21.1 us  [spread(): return lax.psum(kept, axis)]
    all_gather x0 -> x1, waiting for transfers between devices: none -> 37.3 us  [local(): images = lax.all_gather(images, 'pair', axis=1, tiled=True)]
    unnamed x4, waiting for transfers between devices: 303 us -> 334 us
    unnamed x10 -> x7, local copies, waits for them, and re-layouts: 31.6 us -> 9.05 us
    all_to_all x1 -> x0, local copies, waits for them, and re-layouts: 22.3 us -> none  [local(): lax.all_to_all(pair_conduction, 'pair', split_axis=1, concat_axis=0, tile...]
    all_to_all x1 -> x0, waiting for transfers between devices: 19.7 us -> none  [local(): lax.all_to_all(pair_conduction, 'pair', split_axis=1, concat_axis=0, tile...]
    psum x1, blocking collectives: 27.1 us -> 7.96 us  [local(): images = lax.psum(slab, 'ga').astype(jnp.bfloat16)]
  transfers between devices with their start and end apart: 4 -> 3, of which waited for: 4 -> 3; matrix products, arithmetic and copies ran while one was open for 6% -> 7% of each run, Pallas kernels for 0% -> 0%
where the time goes in v1:
time: 449 us; the launch traced here: 447 us
  waiting for transfers between devices  392 us (87%)
  matrix products  20.7 us (5%)
  between operations  15.5 us (3%)
  local copies, waits for them, and re-layouts  9.05 us (2%)
  blocking collectives  7.96 us (2%)
    unnamed x4, waiting for transfers between devices  334 us
    all_gather x1, waiting for transfers between devices, local(): images = lax.all_gather(images, 'pair', axis=1, tiled=True)  37.3 us
    psum x1, waiting for transfers between devices, spread(): return lax.psum(kept, axis)  21.1 us
    dot_general x1, matrix products, local(): jnp.einsum('ck,vk->cv', pair_conduction, images, preferred_element_type=j...  12.3 us
    unnamed x7, local copies, waits for them, and re-layouts  9.05 us
  transfers between devices with their start and end apart: 3, of which 3 were waited for; matrix products, arithmetic and copies ran while one was open for 7% of the time, Pallas kernels for 0%

profile of v1, /device:TPU:32, one launch (start us, length us, event | category | flops | bytes accessed | tf_op | source)
XLA Modules:
  0.0 447.5 jit_solution(2211773091940146192)
XLA Ops:
  8.0 0.0 copy-start
  8.0 0.0 copy-start.1
  8.0 0.0 copy-start.2
  8.0 0.0 all-reduce.2.cloned.1.call-start
  8.1 1.8 slice_select_fusion
  9.9 0.0 all-reduce.2.cloned.1.call-update
  9.9 0.0 all-gather.2.cloned.1.call-start
  10.0 0.0 copy-done
  10.0 3.0 fusion.1
  13.0 8.0 %psum.14 = bf16[64,256]{1,0:T(8,128)(2,1)} all-reduce(f32[64,256]{1,0:T(8,128)S(1)} %fusion.1), channel_id=1, replica_groups=mesh['pair'=64,'ga'=2] {'ga'}, use_global_device_ids=true, to_apply=%region_0.0 | all-reduce | flops 16384 | bytes 98304 | tf_op jit(solution)/shard_map/psum | solution.py:17
  21.0 0.0 all-gather.2.cloned.1.call-update
  21.0 0.0 reduce-scatter.4.cloned.1.call-start
  21.0 21.1 %all-reduce.2.cloned.1.call-done = bf16[512,256]{1,0:T(8,128)(2,1)} async-done(((bf16[512,256]{1,0:T(8,128)(2,1)}), bf16[512,256]{1,0:T(8,128)(2,1)}) %all-reduce.2.cloned.1.call-update) | async-done | bytes 262160 | tf_op jit(solution)/shard_map/psum | solution.py:12
  42.1 0.0 copy-done.1
  42.2 0.0 copy-done.2
  42.2 5.5 %convolution_bitcast_fusion = f32[4096,512]{0,1:T(8,128)} fusion(bf16[4096,256]{1,0:T(8,128)(2,1)S(1)} %copy-done.1, bf16[512,256]{1,0:T(8,128)(2,1)} %all-reduce.2.cloned.1.call-done, f32[256]{0:T(256)S(1)} %copy-done.2), kind=kOutput, calls=%fused_computation | convolution fusion | flops 1074135040 | bytes 10748928 | tf_op jit(solution)/shard_map/gk,xk->gx/dot_general | solution.py:26
  47.6 9.0 %copy.9 = f32[4096,512]{1,0:T(8,128)} copy(f32[4096,512]{0,1:T(8,128)} %convolution_bitcast_fusion) | data formatting | bytes 16777216
  56.7 0.0 reduce-scatter.4.cloned.1.call-update
  56.7 37.3 %all-gather.2.cloned.1.call-done = bf16[64,16384]{1,0:T(8,128)(2,1)} async-done(((bf16[64,256]{1,0:T(8,128)(2,1)}), bf16[64,16384]{1,0:T(8,128)(2,1)}) %all-gather.2.cloned.1.call-update) | async-done | bytes 2097168 | tf_op jit(solution)/shard_map/all_gather | solution.py:18
  94.0 12.3 %convolution_bitcast_fusion.1 = f32[512,64]{0,1:T(8,128)} fusion(bf16[64,16384]{1,0:T(8,128)(2,1)} %all-gather.2.cloned.1.call-done, bf16[512,16384]{1,0:T(8,128)(2,1)} %param.7), kind=kOutput, calls=%fused_computation.1 | convolution fusion | flops 1073741824 | bytes 19005440 | tf_op jit(solution)/shard_map/ck,vk->cv/dot_general | solution.py:19
  106.2 333.8 %reduce-scatter.4.cloned.1.call-done = f32[64,512]{1,0:T(8,128)} async-done(((f32[4096,512]{1,0:T(8,128)}), f32[64,512]{1,0:T(8,128)}) %reduce-scatter.4.cloned.1.call-update) | async-done | bytes 131088
Async XLA Ops:
  8.0 2.0 copy-start
  8.0 34.1 %copy-start.1 = (bf16[4096,256]{1,0:T(8,128)(2,1)S(1)}, bf16[4096,256]{1,0:T(8,128)(2,1)}, u32[]{:S(2)}) copy-start(bf16[4096,256]{1,0:T(8,128)(2,1)} %param.8) | copy-start | bytes 6291460
  8.0 34.1 %copy-start.2 = (f32[256]{0:T(256)S(1)}, f32[256]{0:T(256)}, u32[]{:S(2)}) copy-start(f32[256]{0:T(256)} %param.9) | copy-start | bytes 3076
  8.0 34.1 %all-reduce.2.cloned.1.call-start = ((), (), s32[]{:S(2)}) async-start(), calls=%async_computation.2 | async-start | bytes 524288 | tf_op jit(solution)/shard_map/psum | solution.py:12
  9.9 84.0 %all-gather.2.cloned.1.call-start = ((), (), s32[]{:S(2)}) async-start(), calls=%async_computation.1 | async-start | bytes 2129920 | tf_op jit(solution)/shard_map/all_gather | solution.py:18
  21.0 419.1 %reduce-scatter.4.cloned.1.call-start = ((), (), s32[]{:S(2)}) async-start(), calls=%async_computation.3 | async-start | bytes 8519680
Sparse Core Ops, SparseCore 0:
  11.3 30.8 all-reduce.1
Sparse Core Ops, SparseCore 1:
  21.1 72.9 all-gather.1
  96.9 343.1 reduce-scatter.3

commit v2 on v1

v2 whole, which is shorter than its diff:
```python
import jax
import jax.numpy as jnp
from jax import lax
from jax.experimental import pallas as pl
from jax.experimental.pallas import tpu as pltpu
from jax.sharding import PartitionSpec as P

MESH = pl.DeviceIdType.MESH
BF = jnp.bfloat16
F32 = jnp.float32
KB = 256
MESSAGES = 96


def dot_t(a, b):
    return lax.dot_general(a, b, (((1,), (1,)), ((), ())), preferred_element_type=F32)


def kernel(
    pv_hbm,
    w_hbm,
    pc_hbm,
    pm_hbm,
    cl_hbm,
    direct_ref,
    exchange_ref,
    pv_buf,
    w_buf,
    pc_buf,
    a_buf,
    b_buf,
    win_buf,
    cl_buf,
    part_buf,
    part_recv,
    img,
    snd1,
    opp_recv,
    dir_recv,
    comb_recv,
    acc1,
    snd2,
    recv2,
    acc2,
    snd3,
    recv3,
    load_sem,
    ss,
    rs,
):
    pair = lax.axis_index("pair")
    ga = lax.axis_index("ga")
    c = pair % 2
    y = (pair // 2) % 4
    zh = (pair // 8) % 2
    x = pair // 16
    z = zh * 2 + ga

    def dev(dx=0, dy=0, dz=0, dc=0):
        xx, yy, zz, cc = (x + dx) % 4, (y + dy) % 4, (z + dz) % 4, (c + dc) % 2
        return {"pair": ((xx * 2 + zz // 2) * 4 + yy) * 2 + cc, "ga": zz % 2}

    core_peer = dev(dc=1)
    ga_peer = {"pair": pair, "ga": 1 - ga}
    z_half = dev(dz=2)
    peers = [core_peer] + [dev(**{d: o}) for d in ("dx", "dy", "dz") for o in (1, 2, 3)]

    count = [0]
    sent = []

    def message(src, dst, device):
        i = count[0]
        count[0] += 1
        copy = pltpu.make_async_remote_copy(
            src_ref=src,
            dst_ref=dst,
            send_sem=ss.at[i],
            recv_sem=rs.at[i],
            device_id=device,
            device_id_type=MESH,
        )
        return copy

    def send(copy):
        copy.start()
        sent.append(copy)

    loads = [0]

    def load(src, dst):
        i = loads[0]
        loads[0] += 1
        return pltpu.make_async_copy(src, dst, load_sem.at[i])

    barrier = pltpu.get_barrier_semaphore()
    for peer in peers:
        pl.semaphore_signal(barrier, inc=1, device_id=peer, device_id_type=MESH)

    ld_win = load(pm_hbm.at[0, 0], win_buf)
    ld_cl = load(cl_hbm, cl_buf)
    ld_pv = load(pv_hbm, pv_buf)
    ld_w = [load(w_hbm.at[pl.ds(k * 2048, 2048)], w_buf.at[pl.ds(k * 2048, 2048)]) for k in range(4)]
    ld_a = load(pm_hbm.at[:, :, :, c], a_buf.at[c])
    ld_pc = [load(pc_hbm.at[pl.ds(k * 128, 128)], pc_buf.at[pl.ds(k * 128, 128)]) for k in range(4)]

    @pl.when(ga == 0)
    def _():
        ld_win.start()

    ld_cl.start()
    ld_pv.start()
    for copy in ld_w:
        copy.start()
    ld_a.start()

    pl.semaphore_wait(barrier, len(peers))

    m_a = message(pm_hbm.at[:, :, :, 1 - c], a_buf.at[c], core_peer)
    send(m_a)

    m_b_ga = [message(b_buf.at[c, n], b_buf.at[c, n], ga_peer) for n in range(2)]
    m_b_core = [message(b_buf.at[c, n], b_buf.at[c, n], core_peer) for n in range(2)]

    @pl.when(ga == 0)
    def _():
        ld_win.wait()

    ld_cl.wait()

    @pl.when(ga == 0)
    def _():
        v = cl_buf[...]
        for n in range(2):
            rows = win_buf[2 * n : 2 * n + 2].reshape(256, KB)
            b_buf[c, n] = (rows.astype(F32) * v).astype(BF)
            m_b_ga[n].start()
            m_b_core[n].start()

    ld_pv.wait()
    part = None
    for k in range(4):
        ld_w[k].wait()
        term = jnp.dot(
            pv_buf[:, k * 2048 : (k + 1) * 2048],
            w_buf[k * 2048 : (k + 1) * 2048, :],
            preferred_element_type=F32,
        )
        part = term if part is None else part + term
    part_buf[...] = part.reshape(2, 32, KB)
    m_part = message(part_buf.at[1 - ga], part_recv, ga_peer)
    send(m_part)
    for copy in ld_pc:
        copy.start()

    ld_a.wait()

    def tile_rows(s, r, d, h):
        rows = pl.ds(r * 32, 32)
        if r == 0:
            value = a_buf[s, (x + d) % 4, h, :, rows, :]
        else:
            value = a_buf[s, :, h, (y + d) % 4, rows, :]
        return value.reshape(128, KB)

    def tile(r, n, d, halves):
        total = None
        for s in range(2):
            rows = [tile_rows(s, r, d, h) for h in halves]
            rows = rows[0] if len(rows) == 1 else jnp.concatenate(rows, axis=0)
            term = dot_t(rows, b_buf[s, n])
            total = term if total is None else total + term
        return total.reshape(len(halves), 4, 32, 256)

    def first(r, d):
        return dev(dx=d) if r == 0 else dev(dy=d)

    def second(r, d):
        return dev(dy=d) if r == 0 else dev(dx=d)

    streams = [(r, n) for n in range(2) for r in range(2)]
    m_opp, m_dir, m_comb, m_two, m_three = {}, {}, {}, {}, {}
    for r, n in streams:
        for way, d in ((0, 1), (1, 3)):
            m_opp[r, n, way] = message(snd1.at[r, n, 0, way], opp_recv.at[r, n, way], first(r, d))
            m_dir[r, n, way] = message(snd1.at[r, n, 1, way], dir_recv.at[r, n, way], first(r, d))
            m_comb[r, n, way] = message(snd1.at[r, n, 2, way], comb_recv.at[r, n, way], first(r, d))
        for e in (1, 2, 3):
            m_two[r, n, e] = message(snd2.at[r, n, e - 1], recv2.at[r, n, e - 1], second(r, e))
        m_three[r, n] = message(snd3.at[r, n], recv3.at[r, n], z_half)

    def rs_open(n):
        for r in range(2):
            snd1[r, n, 0] = tile(r, n, 2, (0, 1)).astype(BF)
            m_opp[r, n, 0].start()
            m_opp[r, n, 1].start()
        for r in range(2):
            snd1[r, n, 1, 0] = tile(r, n, 1, (1,))[0].astype(BF)
            m_dir[r, n, 0].start()
            snd1[r, n, 1, 1] = tile(r, n, 3, (0,))[0].astype(BF)
            m_dir[r, n, 1].start()

    def rs_comb(n):
        for r in range(2):
            for way, d, h in ((0, 1, 0), (1, 3, 1)):
                own = tile(r, n, d, (h,))[0]
                m_opp[r, n, way].wait_recv()
                snd1[r, n, 2, way] = (own + opp_recv[r, n, way].astype(F32)).astype(BF)
                m_comb[r, n, way].start()
        for r in range(2):
            acc1[r, n] = tile(r, n, 0, (0, 1))

    def rs_second(n):
        for r in range(2):
            for way in range(2):
                m_dir[r, n, way].wait_recv()
            for way in range(2):
                m_comb[r, n, way].wait_recv()
            for h in range(2):
                acc1[r, n, h] = acc1[r, n, h] + dir_recv[r, n, 1 - h].astype(F32) + comb_recv[r, n, h].astype(F32)
            me = y if r == 0 else x
            for e in (2, 1, 3):
                snd2[r, n, e - 1] = acc1[r, n, :, (me + e) % 4].astype(BF)
                m_two[r, n, e].start()

    def rs_third(n):
        for r in range(2):
            me = y if r == 0 else x
            for e in (1, 3, 2):
                m_two[r, n, e].wait_recv()
            total = acc1[r, n, :, me]
            for e in (1, 3, 2):
                total = total + recv2[r, n, e - 1].astype(F32)
            acc2[r, n] = total
            snd3[r, n] = acc2[r, n, 1 - zh].astype(BF)
            m_three[r, n].start()

    def rs_last(n):
        for r in range(2):
            m_three[r, n].wait_recv()
            exchange_ref[r * 32 : r * 32 + 32, n * 256 : n * 256 + 256] = acc2[r, n, zh] + recv3[r, n].astype(F32)

    m_z = [message(img.at[c, zh, x, y, ga], img.at[c, zh, x, y, ga], dev(dz=f)) for f in (1, 2, 3)]

    def gather_axis(h, d):
        return dev(dx=d) if h == 0 else dev(dy=d)

    def gather_second(h, d):
        return dev(dy=d) if h == 0 else dev(dx=d)

    def line(cc, h, e):
        return img.at[cc, h, :, (y + e) % 4] if h == 0 else img.at[cc, h, (x + e) % 4]

    def half_line(cc, h, e, part):
        some = pl.ds(2 * part, 2)
        return img.at[cc, h, some, (y + e) % 4] if h == 0 else img.at[cc, h, (x + e) % 4, some]

    m_g1, m_g2, m_relay, m_fwd = {}, {}, {}, {}
    for h in range(2):
        mine = img.at[c, h, x, y]
        for d in (1, 2, 3):
            m_g1[h, d] = message(mine, mine, gather_axis(h, d))
        for d in (1, 3):
            m_g2[h, d] = message(line(c, h, 0), line(c, h, 0), gather_second(h, d))
        m_relay[h, 1] = message(half_line(c, h, 3, 0), half_line(c, h, 3, 0), gather_second(h, 1))
        m_relay[h, 3] = message(half_line(c, h, 1, 1), half_line(c, h, 1, 1), gather_second(h, 3))
        for e in range(4):
            m_fwd[h, e] = message(line(c, h, e), line(c, h, e), core_peer)

    def direct_group(cc, h, e, begin=False):
        total = None
        for j in range(4):
            xx, yy = (j, (y + e) % 4) if h == 0 else ((x + e) % 4, j)
            block = ((xx * 2 + h) * 4 + yy) * 2 + cc
            cols = pl.ds(pl.multiple_of(block * KB, KB), KB)
            term = dot_t(pc_buf[:, cols], img[cc, h, xx, yy].reshape(64, KB))
            total = term if total is None else total + term
        direct_ref[...] = total if begin else direct_ref[...] + total

    m_a.wait_recv()

    @pl.when(ga == 0)
    def _():
        m_b_core[0].wait_recv()
        rs_open(0)

    m_part.wait_recv()
    img[c, zh, x, y, ga] = (part_buf[ga] + part_recv[...]).astype(BF)
    for copy in m_z:
        send(copy)

    @pl.when(ga == 1)
    def _():
        m_b_ga[0].wait_recv()
        m_b_core[0].start()

    for copy in m_z:
        copy.wait_recv()
    for h in range(2):
        for d in (2, 1, 3):
            send(m_g1[h, d])

    @pl.when(ga == 1)
    def _():
        m_b_core[0].wait_recv()
        rs_open(0)

    for h in range(2):
        for d in (1, 3, 2):
            m_g1[h, d].wait_recv()
        for d in (1, 3):
            send(m_g2[h, d])
    for h in range(2):
        send(m_fwd[h, 0])

    rs_comb(0)

    @pl.when(ga == 1)
    def _():
        m_b_ga[1].wait_recv()
        m_b_core[1].start()

    m_b_core[1].wait_recv()
    rs_open(1)

    for h in range(2):
        for d in (1, 3):
            m_g2[h, d].wait_recv()
            send(m_relay[h, d])
    for h in range(2):
        for e in (1, 3):
            send(m_fwd[h, e])

    rs_second(0)
    rs_comb(1)

    for copy in ld_pc:
        copy.wait()
    for h in range(2):
        direct_group(c, h, 0, begin=h == 0)
    for h in range(2):
        m_fwd[h, 0].wait_recv()
        direct_group(1 - c, h, 0)

    rs_third(0)

    for h in range(2):
        for d in (1, 3):
            m_relay[h, d].wait_recv()
        send(m_fwd[h, 2])
    for h in range(2):
        for e in (1, 3):
            direct_group(c, h, e)

    rs_second(1)

    for h in range(2):
        for e in (1, 3):
            m_fwd[h, e].wait_recv()
            direct_group(1 - c, h, e)

    rs_last(0)
    rs_third(1)

    for h in range(2):
        direct_group(c, h, 2)
        m_fwd[h, 2].wait_recv()
        direct_group(1 - c, h, 2)

    rs_last(1)

    for copy in sent:
        copy.wait_send()

    @pl.when(ga == 0)
    def _():
        for n in range(2):
            m_b_ga[n].wait_send()

    for n in range(2):
        m_b_core[n].wait_send()
    for group in (m_opp, m_dir, m_comb, m_two, m_three):
        for copy in group.values():
            copy.wait_send()


def solution(mesh):
    def local(pair_valence, screened, pair_conduction, pair_mixed, coulomb):
        anywhere = pl.BlockSpec(memory_space=pl.ANY)
        vmem = pl.BlockSpec(memory_space=pltpu.VMEM)
        return pl.pallas_call(
            kernel,
            out_shape=(
                jax.ShapeDtypeStruct((512, 64), F32),
                jax.ShapeDtypeStruct((64, 512), F32),
            ),
            in_specs=[anywhere] * 5,
            out_specs=(vmem, vmem),
            scratch_shapes=[
                pltpu.VMEM((64, 8192), BF),
                pltpu.VMEM((8192, KB), BF),
                pltpu.VMEM((512, 16384), BF),
                pltpu.VMEM((2, 4, 2, 4, 64, KB), BF),
                pltpu.VMEM((2, 2, 256, KB), BF),
                pltpu.VMEM((4, 2, 64, KB), BF),
                pltpu.VMEM((1, KB), F32),
                pltpu.VMEM((2, 32, KB), F32),
                pltpu.VMEM((32, KB), F32),
                pltpu.VMEM((2, 2, 4, 4, 2, 32, KB), BF),
                pltpu.VMEM((2, 2, 3, 2, 4, 32, 256), BF),
                pltpu.VMEM((2, 2, 2, 4, 32, 256), BF),
                pltpu.VMEM((2, 2, 2, 4, 32, 256), BF),
                pltpu.VMEM((2, 2, 2, 4, 32, 256), BF),
                pltpu.VMEM((2, 2, 2, 4, 32, 256), F32),
                pltpu.VMEM((2, 2, 3, 2, 32, 256), BF),
                pltpu.VMEM((2, 2, 3, 2, 32, 256), BF),
                pltpu.VMEM((2, 2, 2, 32, 256), F32),
                pltpu.VMEM((2, 2, 32, 256), BF),
                pltpu.VMEM((2, 2, 32, 256), BF),
                pltpu.SemaphoreType.DMA((16,)),
                pltpu.SemaphoreType.DMA((MESSAGES,)),
                pltpu.SemaphoreType.DMA((MESSAGES,)),
            ],
            compiler_params=pltpu.CompilerParams(
                collective_id=0, has_side_effects=True, vmem_limit_bytes=60 << 20
            ),
            cost_estimate=pl.CostEstimate(flops=3 << 30, bytes_accessed=24 << 20, transcendentals=0),
        )(
            pair_valence,
            screened,
            pair_conduction,
            pair_mixed.reshape(4, 2, 4, 2, 64, KB),
            coulomb.reshape(1, KB),
        )

    return jax.shard_map(
        local,
        mesh=mesh,
        in_specs=(
            P(None, "ga"),
            P("ga", "pair"),
            P(("pair", "ga"), None),
            P("ga", "pair"),
            P("pair"),
        ),
        out_specs=(P(("pair", "ga"), None), P(("ga", "pair"), None)),
        check_vma=False,
    )
```

time: 449 us -> 49.5 us (0.11)
  waiting for transfers between devices: 392 us -> 0 us
  Pallas kernels: 0 us -> 44.8 us
  matrix products: 20.7 us -> 0 us
  between operations: 15.5 us -> 0.64 us
  blocking collectives: 7.96 us -> 0 us
  local copies, waits for them, and re-layouts: 9.05 us -> 3.29 us
    unnamed x4 -> x0, waiting for transfers between devices: 334 us -> none
    pallas_call x0 -> x1, Pallas kernels: none -> 44.8 us  [local(): pl.pallas_call(kernel, out_shape=(jax.ShapeDtypeStruct((512, 64), F32), j...]
    all_gather x1 -> x0, waiting for transfers between devices: 37.3 us -> none  [local(): images = lax.all_gather(images, 'pair', axis=1, tiled=True)]
    psum x1 -> x0, waiting for transfers between devices: 21.1 us -> none  [spread(): return lax.psum(kept, axis)]
    dot_general x3 -> x0, matrix products: 20.7 us -> none  [the longest x1 12.3 us: local(): jnp.einsum('ck,vk->cv', pair_conduction, images, preferred_element_type=j...]
    psum x1 -> x0, blocking collectives: 7.96 us -> none  [local(): images = lax.psum(slab, 'ga').astype(jnp.bfloat16)]
    unnamed x7 -> x1, local copies, waits for them, and re-layouts: 9.05 us -> 1.57 us
  transfers between devices with their start and end apart: 3 -> 0, of which waited for: 3 -> 0; matrix products, arithmetic and copies ran while one was open for 7% -> 0% of each run, Pallas kernels for 0% -> 0%
where the time goes in v2:
time: 49.5 us; the launch traced here: 48.7 us
  Pallas kernels  44.8 us (91%)
  local copies, waits for them, and re-layouts  3.29 us (7%)
  between operations  0.64 us (1%)
    pallas_call x1, Pallas kernels, local(): pl.pallas_call(kernel, out_shape=(jax.ShapeDtypeStruct((512, 64), F32), j...  44.8 us
    pallas_call x1, local copies, waits for them, and re-layouts, local(): pl.pallas_call(kernel, out_shape=(jax.ShapeDtypeStruct((512, 64), F32), j...  1.72 us
    unnamed x1, local copies, waits for them, and re-layouts  1.57 us

profile of v2, /device:TPU:32, one launch (start us, length us, event | category | flops | bytes accessed | tf_op | source)
XLA Modules:
  0.0 48.7 jit_solution(17155394344712242637)
XLA Ops:
  0.6 44.8 %shard_map.68 = (f32[512,64]{1,0:T(8,128)}, f32[64,512]{1,0:T(8,128)}) custom-call(bf16[64,8192]{1,0:T(8,128)(2,1)} %pv_hbm.1, bf16[8192,256]{1,0:T(8,128)(2,1)} %w_hbm.1, bf16[512,16384]{1,0:T(8,128)(2,1)} %pc_hbm.1, bf16[4,2,4,2,64,256]{5,4,3,2,1,0:T(8,128)(2,1)} %bitcast.2, f32[1,256]{1,0:T(1,128)} %bitcast.3), custom_call_target="tpu_custom_call" | custom-call | flops 3221225472 | bytes 25165824 | tf_op jit(solution)/shard_map/pallas_call | solution.py:390
  45.4 1.7 %copy.7 = f32[512,64]{0,1:T(8,128)} copy(f32[512,64]{1,0:T(8,128)} %get-tuple-element.2) | data formatting | bytes 262144 | tf_op jit(solution)/shard_map/pallas_call | solution.py:390
  47.1 1.6 %copy.9 = f32[64,512]{1,0:T(8,128)} copy(f32[64,512]{1,0:T(8,128)} %get-tuple-element.7) | data formatting | bytes 262144

commit v3 on v1

v3 whole, which is shorter than its diff:
```python
import jax
import jax.numpy as jnp
from jax import lax
from jax.experimental import pallas as pl
from jax.experimental.pallas import tpu as pltpu
from jax.sharding import PartitionSpec as P

MESH = pl.DeviceIdType.MESH
BF = jnp.bfloat16
F32 = jnp.float32
KB = 256
CHUNKS = 4
W = 512 // CHUNKS


def dot_t(a, b):
    return lax.dot_general(a, b, (((1,), (1,)), ((), ())), preferred_element_type=F32)


def kernel(
    pv_hbm,
    w_hbm,
    pc_hbm,
    pm_hbm,
    cl_hbm,
    direct_ref,
    exchange_ref,
    pv_buf,
    w_buf,
    pc_buf,
    a_buf,
    b_buf,
    win_buf,
    cl_buf,
    part_buf,
    part_recv,
    img,
    snd1,
    opp_recv,
    near_recv,
    acc1,
    snd2,
    recv2,
    dacc,
    load_sem,
    send_sem,
    b_sem,
    rs_sem,
    g_sem,
):
    pair = lax.axis_index("pair")
    ga = lax.axis_index("ga")
    c = pair % 2
    y = (pair // 2) % 4
    zh = (pair // 8) % 2
    x = pair // 16
    z = zh * 2 + ga

    def dev(dx=0, dy=0, dz=0, dc=0):
        xx, yy, zz, cc = (x + dx) % 4, (y + dy) % 4, (z + dz) % 4, (c + dc) % 2
        return {"pair": ((xx * 2 + zz // 2) * 4 + yy) * 2 + cc, "ga": zz % 2}

    core_peer = dev(dc=1)
    ga_peer = {"pair": pair, "ga": 1 - ga}
    others = [(e, f) for e in range(4) for f in range(2) if (e, f) != (0, 0)]
    peers = [core_peer] + [dev(dz=o) for o in (1, 2, 3)]
    for f in range(2):
        for e in (1, 2, 3):
            peers += [dev(dx=e, dz=2 * f), dev(dy=e, dz=2 * f)]

    def send(src, dst, device, s_sem, r_sem):
        pltpu.make_async_remote_copy(
            src_ref=src,
            dst_ref=dst,
            send_sem=s_sem,
            recv_sem=r_sem,
            device_id=device,
            device_id_type=MESH,
        ).start()

    def wait(ref, sem):
        pltpu.make_async_copy(ref, ref, sem).wait()

    S_PART, S_A, S_BCORE, S_BGA, S_ONE, S_TWO, S_Z, S_G1, S_G2, S_RELAY, S_FWD = (send_sem.at[i] for i in range(11))
    R_PART, R_Z = g_sem.at[0], g_sem.at[1]

    barrier = pltpu.get_barrier_semaphore()
    for peer in peers:
        pl.semaphore_signal(barrier, inc=1, device_id=peer, device_id_type=MESH)

    ld_win = pltpu.make_async_copy(pm_hbm.at[0, 0], win_buf, load_sem.at[0])
    ld_cl = pltpu.make_async_copy(cl_hbm, cl_buf, load_sem.at[1])
    ld_pv = pltpu.make_async_copy(pv_hbm, pv_buf, load_sem.at[2])
    ld_a = pltpu.make_async_copy(pm_hbm.at[:, :, :, c], a_buf.at[c], load_sem.at[3])
    ld_pc = pltpu.make_async_copy(pc_hbm, pc_buf, load_sem.at[4])
    ld_w = [
        pltpu.make_async_copy(w_hbm.at[pl.ds(k * 2048, 2048)], w_buf.at[pl.ds(k * 2048, 2048)], load_sem.at[5 + k])
        for k in range(4)
    ]

    @pl.when(ga == 0)
    def _():
        ld_win.start()

    ld_cl.start()
    ld_pv.start()
    for copy in ld_w:
        copy.start()
    ld_a.start()

    ld_cl.wait()

    @pl.when(ga == 0)
    def _():
        ld_win.wait()
        v = cl_buf[...]
        for n in range(CHUNKS):
            rows = win_buf[n].reshape(W, KB)
            b_buf[c, n] = (rows.astype(F32) * v).astype(BF)

    ld_pv.wait()
    part = None
    for k in range(4):
        ld_w[k].wait()
        term = jnp.dot(
            pv_buf[:, k * 2048 : (k + 1) * 2048],
            w_buf[k * 2048 : (k + 1) * 2048, :],
            preferred_element_type=F32,
        )
        part = term if part is None else part + term
    part_buf[...] = part.reshape(2, 32, KB)

    pl.semaphore_wait(barrier, len(peers))

    send(part_buf.at[1 - ga], part_recv, ga_peer, S_PART, R_PART)

    def b_to_core(n):
        send(b_buf.at[c, n], b_buf.at[c, n], core_peer, S_BCORE, b_sem.at[0, n])

    def b_wait(n):
        wait(b_buf.at[1 - c, n], b_sem.at[0, n])

    def a_to_core(r):
        rows = pl.ds(r * 32, 32)
        send(pm_hbm.at[:, :, :, 1 - c, rows], a_buf.at[c, :, :, :, rows], core_peer, S_A, b_sem.at[2, r])

    def a_wait(r):
        wait(a_buf.at[1 - c, :, :, :, pl.ds(r * 32, 32)], b_sem.at[2, r])

    @pl.when(ga == 0)
    def _():
        for n in range(CHUNKS):
            send(b_buf.at[c, n], b_buf.at[c, n], ga_peer, S_BGA, b_sem.at[1, n])
        for n in range(CHUNKS):
            b_to_core(n)

    for r in range(2):
        a_to_core(r)

    def tile_rows(s, r, d, h):
        rows = pl.ds(r * 32, 32)
        if r == 0:
            value = a_buf[s, (x + d) % 4, h, :, rows, :]
        else:
            value = a_buf[s, :, h, (y + d) % 4, rows, :]
        return value.reshape(128, KB)

    def tile(r, n, parts):
        total = None
        for s in range(2):
            rows = jnp.concatenate([tile_rows(s, r, d, h) for d, h in parts], axis=0)
            term = dot_t(rows, b_buf[s, n])
            total = term if total is None else total + term
        return total.reshape(len(parts), 4, 32, W)

    def first(r, way):
        d = 1 if way == 0 else 3
        return dev(dx=d) if r == 0 else dev(dy=d)

    def second(r, e, f):
        return dev(dy=e, dz=2 * f) if r == 0 else dev(dx=e, dz=2 * f)

    def rs_opp(r, n):
        snd1[r, n, 0] = tile(r, n, ((2, 0), (2, 1))).astype(BF)
        for way in range(2):
            send(snd1.at[r, n, 0, way], opp_recv.at[r, n, way], first(r, way), S_ONE, rs_sem.at[0, r, n])

    def rs_dir(r, n):
        snd1[r, n, 1] = tile(r, n, ((1, 1), (3, 0))).astype(BF)
        for way in range(2):
            send(snd1.at[r, n, 1, way], near_recv.at[r, n, way], first(r, way), S_ONE, rs_sem.at[1, r, n])

    def rs_comb(n):
        for r in range(2):
            own = tile(r, n, ((1, 0), (3, 1)))
            wait(opp_recv.at[r, n], rs_sem.at[0, r, n])
            for way in range(2):
                snd1[r, n, 2, way] = (own[way] + opp_recv[r, n, way].astype(F32)).astype(BF)
                send(snd1.at[r, n, 2, way], near_recv.at[r, n, 2 + way], first(r, way), S_ONE, rs_sem.at[1, r, n])
        for r in range(2):
            acc1[r, n] = tile(r, n, ((0, 0), (0, 1)))

    def rs_second(n):
        for r in range(2):
            wait(near_recv.at[r, n], rs_sem.at[1, r, n])
            for h in range(2):
                acc1[r, n, h] = (
                    acc1[r, n, h] + near_recv[r, n, 1 - h].astype(F32) + near_recv[r, n, 2 + h].astype(F32)
                )
            me = y if r == 0 else x
            for k, (e, f) in enumerate(others):
                hh = zh if f == 0 else 1 - zh
                snd2[r, n, k] = acc1[r, n, hh, (me + e) % 4].astype(BF)
                send(snd2.at[r, n, k], recv2.at[r, n, k], second(r, e, f), S_TWO, rs_sem.at[2, r, n])

    def rs_last(n):
        for r in range(2):
            me = y if r == 0 else x
            total = acc1[r, n, zh, me]
            wait(recv2.at[r, n], rs_sem.at[2, r, n])
            for k in range(len(others)):
                total = total + recv2[r, n, k].astype(F32)
            exchange_ref[r * 32 : r * 32 + 32, n * W : n * W + W] = total

    def slab(h, d, e):
        if h == 0:
            return img.at[c, h, (x + d) % 4, (y + e) % 4]
        return img.at[c, h, (x + e) % 4, (y + d) % 4]

    def line(cc, h, e):
        return img.at[cc, h, :, (y + e) % 4] if h == 0 else img.at[cc, h, (x + e) % 4]

    def along(h, d):
        return dev(dx=d) if h == 0 else dev(dy=d)

    def across(h, e):
        return dev(dy=e) if h == 0 else dev(dx=e)

    def g2_sem(h, e, late):
        return g_sem.at[4 + h * 4 + (e // 2) * 2 + late]

    def slabs(n):
        return img.at[0, 0, 0, pl.ds(0, n)]

    def g_sum():
        wait(part_recv, R_PART)
        img[c, zh, x, y, ga] = (part_buf[ga] + part_recv[...]).astype(BF)
        mine = img.at[c, zh, x, y, ga]
        for f in (2, 1, 3):
            send(mine, mine, dev(dz=f), S_Z, R_Z)

    def g_second_send(h, d):
        for e in (1, 3):
            send(slab(h, d, 0), slab(h, d, 0), across(h, e), S_G2, g2_sem(h, 4 - e, 0 if d == 0 else 1))

    def g_first():
        wait(img.at[0, 0, 0, pl.ds(0, 3), 0], R_Z)
        for h in range(2):
            for d in (2, 1, 3):
                send(slab(h, 0, 0), slab(h, 0, 0), along(h, d), S_G1, g_sem.at[2 + h])
        for h in range(2):
            g_second_send(h, 0)

    def g_second():
        for h in range(2):
            wait(slabs(3), g_sem.at[2 + h])
            for d in (1, 3, 2):
                g_second_send(h, d)
        for h in range(2):
            g_forward(h, 0)

    def g_relay_send(h, d):
        e = 1 if d in (0, 2) else 3
        send(slab(h, d, 4 - e), slab(h, d, 4 - e), across(h, e), S_RELAY, g_sem.at[12 + h])

    def g_relay_own():
        for h in range(2):
            wait(slabs(1), g2_sem(h, 3, 0))
            g_relay_send(h, 0)

    def g_relay():
        for h in range(2):
            wait(slabs(3), g2_sem(h, 1, 1))
            for d in (1, 3):
                g_relay_send(h, d)
            wait(slabs(3), g2_sem(h, 3, 1))
            g_relay_send(h, 2)
            wait(slabs(1), g2_sem(h, 1, 0))

    def g_forward(h, e):
        send(line(c, h, e), line(c, h, e), core_peer, S_FWD, g_sem.at[14 + h * 4 + e])

    def g_forwarded(h, e):
        wait(line(1 - c, h, e), g_sem.at[14 + h * 4 + e])

    def g_last():
        for h in range(2):
            wait(slabs(4), g_sem.at[12 + h])
            g_forward(h, 2)

    def direct_group(cc, h, e, begin=False):
        total = None
        for j in range(4):
            xx, yy = (j, (y + e) % 4) if h == 0 else ((x + e) % 4, j)
            cols = pl.ds(pl.multiple_of((((xx * 2 + h) * 4 + yy) * 2 + cc) * KB, KB), KB)
            term = dot_t(pc_buf[:, cols], img[cc, h, xx, yy].reshape(64, KB))
            total = term if total is None else total + term
        dacc[...] = total if begin else dacc[...] + total

    def fetch(n):
        @pl.when(ga == 1)
        def _():
            wait(b_buf.at[c, n], b_sem.at[1, n])
            b_to_core(n)

    def open_late(n):
        @pl.when(ga == 1)
        def _():
            b_wait(n)
            for r in range(2):
                rs_opp(r, n)
            for r in range(2):
                rs_dir(r, n)

    ld_a.wait()
    a_wait(0)

    @pl.when(ga == 0)
    def _():
        for n in range(CHUNKS):
            b_wait(n)
            rs_opp(0, n)

    a_wait(1)
    ld_pc.start()

    @pl.when(ga == 0)
    def _():
        for n in range(CHUNKS):
            rs_opp(1, n)

    g_sum()

    @pl.when(ga == 0)
    def _():
        for n in range(CHUNKS):
            for r in range(2):
                rs_dir(r, n)

    fetch(0)
    fetch(1)
    open_late(0)
    g_first()
    fetch(2)
    open_late(1)
    fetch(3)
    rs_comb(0)
    open_late(2)
    g_second()
    open_late(3)
    rs_comb(1)
    g_relay_own()
    rs_comb(2)
    rs_second(0)
    g_relay()
    for h in range(2):
        for e in (1, 3):
            g_forward(h, e)
    rs_comb(3)
    rs_second(1)
    ld_pc.wait()
    for h in range(2):
        direct_group(c, h, 0, begin=h == 0)
    for h in range(2):
        g_forwarded(h, 0)
        direct_group(1 - c, h, 0)
    rs_second(2)
    g_last()
    rs_last(0)
    for h in range(2):
        for e in (1, 3):
            direct_group(c, h, e)
    rs_second(3)
    rs_last(1)
    for h in range(2):
        for e in (1, 3):
            g_forwarded(h, e)
            direct_group(1 - c, h, e)
    rs_last(2)
    for h in range(2):
        direct_group(c, h, 2)
        g_forwarded(h, 2)
        direct_group(1 - c, h, 2)
    direct_ref[...] = dacc[...].T
    rs_last(3)

    wait(part_recv, S_PART)
    wait(a_buf.at[0], S_A)
    wait(b_buf.at[0], S_BCORE)

    @pl.when(ga == 0)
    def _():
        wait(b_buf.at[0], S_BGA)

    wait(snd1, S_ONE)
    wait(snd2, S_TWO)
    wait(img.at[0, 0, 0, pl.ds(0, 3), 0], S_Z)
    wait(img.at[0, 0, pl.ds(0, 2), pl.ds(0, 3)], S_G1)
    wait(img.at[0, 0], S_G2)
    wait(img.at[0, 0, pl.ds(0, 2)], S_RELAY)
    wait(img.at[0], S_FWD)


def write_out(a_ref, b_ref, a_out, b_out):
    a_out[...] = a_ref[...]
    b_out[...] = b_ref[...]


def solution(mesh):
    def local(pair_valence, screened, pair_conduction, pair_mixed, coulomb):
        anywhere = pl.BlockSpec(memory_space=pl.ANY)
        vmem = pl.BlockSpec(memory_space=pltpu.VMEM)
        shapes = (jax.ShapeDtypeStruct((64, 512), F32), jax.ShapeDtypeStruct((64, 512), F32))
        direct, exchange = pl.pallas_call(
            kernel,
            out_shape=shapes,
            in_specs=[anywhere] * 5,
            out_specs=(vmem, vmem),
            scratch_shapes=[
                pltpu.VMEM((64, 8192), BF),
                pltpu.VMEM((8192, KB), BF),
                pltpu.VMEM((512, 16384), BF),
                pltpu.VMEM((2, 4, 2, 4, 64, KB), BF),
                pltpu.VMEM((2, CHUNKS, W, KB), BF),
                pltpu.VMEM((4, 2, 64, KB), BF),
                pltpu.VMEM((1, KB), F32),
                pltpu.VMEM((2, 32, KB), F32),
                pltpu.VMEM((32, KB), F32),
                pltpu.VMEM((2, 2, 4, 4, 2, 32, KB), BF),
                pltpu.VMEM((2, CHUNKS, 3, 2, 4, 32, W), BF),
                pltpu.VMEM((2, CHUNKS, 2, 4, 32, W), BF),
                pltpu.VMEM((2, CHUNKS, 4, 4, 32, W), BF),
                pltpu.VMEM((2, CHUNKS, 2, 4, 32, W), F32),
                pltpu.VMEM((2, CHUNKS, 7, 32, W), BF),
                pltpu.VMEM((2, CHUNKS, 7, 32, W), BF),
                pltpu.VMEM((512, 64), F32),
                pltpu.SemaphoreType.DMA((9,)),
                pltpu.SemaphoreType.DMA((11,)),
                pltpu.SemaphoreType.DMA((3, CHUNKS)),
                pltpu.SemaphoreType.DMA((3, 2, CHUNKS)),
                pltpu.SemaphoreType.DMA((22,)),
            ],
            compiler_params=pltpu.CompilerParams(
                collective_id=0, has_side_effects=True, vmem_limit_bytes=60 << 20
            ),
            cost_estimate=pl.CostEstimate(flops=3 << 30, bytes_accessed=24 << 20, transcendentals=0),
        )(
            pair_valence,
            screened,
            pair_conduction,
            pair_mixed.reshape(4, 2, 4, 2, 64, KB),
            coulomb.reshape(1, KB),
        )
        direct, exchange = pl.pallas_call(write_out, out_shape=shapes)(direct, exchange)
        return direct.T, exchange

    return jax.shard_map(
        local,
        mesh=mesh,
        in_specs=(
            P(None, "ga"),
            P("ga", "pair"),
            P(("pair", "ga"), None),
            P("ga", "pair"),
            P("pair"),
        ),
        out_specs=(P(("pair", "ga"), None), P(("ga", "pair"), None)),
        check_vma=False,
    )
```

time: 449 us -> 41.9 us (0.09)
  waiting for transfers between devices: 392 us -> 0 us
  Pallas kernels: 0 us -> 41.1 us
  matrix products: 20.7 us -> 0 us
  between operations: 15.5 us -> 0.64 us
  local copies, waits for them, and re-layouts: 9.05 us -> 0 us
  blocking collectives: 7.96 us -> 0 us
    unnamed x4 -> x0, waiting for transfers between devices: 334 us -> none
    pallas_call x0 -> x2, Pallas kernels: none -> 41.1 us  [the longest x1 39.4 us: local(): pl.pallas_call(kernel, out_shape=shapes, in_specs=[anywhere] * 5, out_spe...]
    all_gather x1 -> x0, waiting for transfers between devices: 37.3 us -> none  [local(): images = lax.all_gather(images, 'pair', axis=1, tiled=True)]
    psum x1 -> x0, waiting for transfers between devices: 21.1 us -> none  [spread(): return lax.psum(kept, axis)]
    dot_general x3 -> x0, matrix products: 20.7 us -> none  [the longest x1 12.3 us: local(): jnp.einsum('ck,vk->cv', pair_conduction, images, preferred_element_type=j...]
    unnamed x7 -> x0, local copies, waits for them, and re-layouts: 9.05 us -> none
    psum x1 -> x0, blocking collectives: 7.96 us -> none  [local(): images = lax.psum(slab, 'ga').astype(jnp.bfloat16)]
  transfers between devices with their start and end apart: 3 -> 0, of which waited for: 3 -> 0; matrix products, arithmetic and copies ran while one was open for 7% -> 0% of each run, Pallas kernels for 0% -> 0%
where the time goes in v3:
time: 41.9 us; the launch traced here: 41.8 us
  Pallas kernels  41.1 us (98%)
  between operations  0.64 us (2%)
    pallas_call x1, Pallas kernels, local(): pl.pallas_call(kernel, out_shape=shapes, in_specs=[anywhere] * 5, out_spe...  39.4 us
    pallas_call x1, Pallas kernels, local(): pl.pallas_call(write_out, out_shape=shapes)(direct, exchange)  1.68 us

profile of v3, /device:TPU:32, one launch (start us, length us, event | category | flops | bytes accessed | tf_op | source)
XLA Modules:
  0.0 41.8 jit_solution(4175192777050911653)
XLA Ops:
  0.6 39.4 %shard_map.68 = (f32[64,512]{1,0:T(8,128)}, f32[64,512]{1,0:T(8,128)}) custom-call(bf16[64,8192]{1,0:T(8,128)(2,1)} %pv_hbm.1, bf16[8192,256]{1,0:T(8,128)(2,1)} %w_hbm.1, bf16[512,16384]{1,0:T(8,128)(2,1)} %pc_hbm.1, bf16[4,2,4,2,64,256]{5,4,3,2,1,0:T(8,128)(2,1)} %bitcast.3, f32[1,256]{1,0:T(1,128)} %bitcast.4), custom_call_target="tpu_custom_call" | custom-call | flops 3221225472 | bytes 25165824 | tf_op jit(solution)/shard_map/pallas_call | solution.py:424
  40.1 1.7 %shard_map.69 = (f32[64,512]{1,0:T(8,128)}, f32[64,512]{1,0:T(8,128)}) custom-call(f32[64,512]{1,0:T(8,128)} %get-tuple-element.6.a_ref, f32[64,512]{1,0:T(8,128)} %get-tuple-element.7.b_ref), custom_call_target="tpu_custom_call" | custom-call | tf_op jit(solution)/shard_map/pallas_call | solution.py:464

commit v4 on v3

--- a/solution.py
+++ b/solution.py
@@ -67,6 +67,7 @@
     for f in range(2):
         for e in (1, 2, 3):
             peers += [dev(dx=e, dz=2 * f), dev(dy=e, dz=2 * f)]
+    peers += [dev(dx=d, dy=e) for d in (1, 2, 3) for e in (1, 2, 3)]
 
     def send(src, dst, device, s_sem, r_sem):
         pltpu.make_async_remote_copy(
@@ -81,7 +82,7 @@
     def wait(ref, sem):
         pltpu.make_async_copy(ref, ref, sem).wait()
 
-    S_PART, S_A, S_BCORE, S_BGA, S_ONE, S_TWO, S_Z, S_G1, S_G2, S_RELAY, S_FWD = (send_sem.at[i] for i in range(11))
+    S_PART, S_A, S_BCORE, S_BGA, S_ONE, S_TWO, S_Z, S_G1, S_G2, S_FWD = (send_sem.at[i] for i in range(10))
     R_PART, R_Z = g_sem.at[0], g_sem.at[1]
 
     barrier = pltpu.get_barrier_semaphore()
@@ -137,25 +138,33 @@
     def b_to_core(n):
         send(b_buf.at[c, n], b_buf.at[c, n], core_peer, S_BCORE, b_sem.at[0, n])
 
+    def b_to_ga(n):
+        send(b_buf.at[c, n], b_buf.at[c, n], ga_peer, S_BGA, b_sem.at[1, n])
+
     def b_wait(n):
         wait(b_buf.at[1 - c, n], b_sem.at[0, n])
 
-    def a_to_core(r):
+    def a_to_core(r, d):
         rows = pl.ds(r * 32, 32)
-        send(pm_hbm.at[:, :, :, 1 - c, rows], a_buf.at[c, :, :, :, rows], core_peer, S_A, b_sem.at[2, r])
-
-    def a_wait(r):
-        wait(a_buf.at[1 - c, :, :, :, pl.ds(r * 32, 32)], b_sem.at[2, r])
-
-    @pl.when(ga == 0)
-    def _():
-        for n in range(CHUNKS):
-            send(b_buf.at[c, n], b_buf.at[c, n], ga_peer, S_BGA, b_sem.at[1, n])
+        if r == 0:
+            src, dst = pm_hbm.at[(x + d) % 4, :, :, 1 - c, rows], a_buf.at[c, (x + d) % 4, :, :, rows]
+        else:
+            src, dst = pm_hbm.at[:, :, (y + d) % 4, 1 - c, rows], a_buf.at[c, :, :, (y + d) % 4, rows]
+        send(src, dst, core_peer, S_A, b_sem.at[2 + r, d])
+
+    def a_wait(r, d):
+        wait(a_buf.at[1 - c, 0, :, :, pl.ds(0, 32)], b_sem.at[2 + r, d])
+
+    @pl.when(ga == 0)
+    def _():
+        for n in (0, 1):
+            b_to_ga(n)
         for n in range(CHUNKS):
             b_to_core(n)
 
-    for r in range(2):
-        a_to_core(r)
+    for d in (2, 1, 3, 0):
+        for r in range(2):
+            a_to_core(r, d)
 
     def tile_rows(s, r, d, h):
         rows = pl.ds(r * 32, 32)
@@ -224,20 +233,20 @@
 
     def slab(h, d, e):
         if h == 0:
-            return img.at[c, h, (x + d) % 4, (y + e) % 4]
-        return img.at[c, h, (x + e) % 4, (y + d) % 4]
-
-    def line(cc, h, e):
-        return img.at[cc, h, :, (y + e) % 4] if h == 0 else img.at[cc, h, (x + e) % 4]
+            return img.at[0, h, (x + d) % 4, (y + e) % 4]
+        return img.at[0, h, (x + e) % 4, (y + d) % 4]
+
+    def line(h, e):
+        return img.at[0, h, :, (y + e) % 4] if h == 0 else img.at[0, h, (x + e) % 4]
+
+    def row(d):
+        return img.at[1, zh, (x + d) % 4, :, ga]
 
     def along(h, d):
         return dev(dx=d) if h == 0 else dev(dy=d)
 
     def across(h, e):
         return dev(dy=e) if h == 0 else dev(dx=e)
-
-    def g2_sem(h, e, late):
-        return g_sem.at[4 + h * 4 + (e // 2) * 2 + late]
 
     def slabs(n):
         return img.at[0, 0, 0, pl.ds(0, n)]
@@ -245,58 +254,84 @@
     def g_sum():
         wait(part_recv, R_PART)
         img[c, zh, x, y, ga] = (part_buf[ga] + part_recv[...]).astype(BF)
-        mine = img.at[c, zh, x, y, ga]
-        for f in (2, 1, 3):
-            send(mine, mine, dev(dz=f), S_Z, R_Z)
+
+        @pl.when(c == 0)
+        def _():
+            mine = img.at[0, zh, x, y, ga]
+            for f in (2, 1, 3):
+                send(mine, mine, dev(dz=f), S_Z, R_Z)
+
+        @pl.when(c == 1)
+        def _():
+            mine = img.at[1, zh, x, y, ga]
+            for d in (0, 2, 1, 3):
+                for e in (0, 2, 1, 3):
+                    if (d, e) != (0, 0):
+                        send(mine, mine, dev(dx=d, dy=e), S_G1, g_sem.at[2 + (4 - d) % 4])
 
     def g_second_send(h, d):
-        for e in (1, 3):
-            send(slab(h, d, 0), slab(h, d, 0), across(h, e), S_G2, g2_sem(h, 4 - e, 0 if d == 0 else 1))
+        for e in (2, 1, 3):
+            send(slab(h, d, 0), slab(h, d, 0), across(h, e), S_G2, g_sem.at[4 + h * 4 + 4 - e])
 
     def g_first():
-        wait(img.at[0, 0, 0, pl.ds(0, 3), 0], R_Z)
-        for h in range(2):
-            for d in (2, 1, 3):
-                send(slab(h, 0, 0), slab(h, 0, 0), along(h, d), S_G1, g_sem.at[2 + h])
-        for h in range(2):
-            g_second_send(h, 0)
+        @pl.when(c == 0)
+        def _():
+            wait(img.at[0, 0, 0, pl.ds(0, 3), 0], R_Z)
+            for h in range(2):
+                for d in (2, 1, 3):
+                    send(slab(h, 0, 0), slab(h, 0, 0), along(h, d), S_G1, g_sem.at[2 + h])
+            for h in range(2):
+                g_second_send(h, 0)
+
+        @pl.when(c == 1)
+        def _():
+            for d in (0, 1, 3, 2):
+                wait(img.at[0, 0, 0, pl.ds(0, 4 if d else 3), 0], g_sem.at[2 + d])
+                for f in (2, 1, 3):
+                    send(row(d), row(d), dev(dz=f), S_Z, g_sem.at[6 + f])
+            p_forward(0)
 
     def g_second():
-        for h in range(2):
-            wait(slabs(3), g_sem.at[2 + h])
-            for d in (1, 3, 2):
-                g_second_send(h, d)
-        for h in range(2):
-            g_forward(h, 0)
-
-    def g_relay_send(h, d):
-        e = 1 if d in (0, 2) else 3
-        send(slab(h, d, 4 - e), slab(h, d, 4 - e), across(h, e), S_RELAY, g_sem.at[12 + h])
-
-    def g_relay_own():
-        for h in range(2):
-            wait(slabs(1), g2_sem(h, 3, 0))
-            g_relay_send(h, 0)
-
-    def g_relay():
-        for h in range(2):
-            wait(slabs(3), g2_sem(h, 1, 1))
-            for d in (1, 3):
-                g_relay_send(h, d)
-            wait(slabs(3), g2_sem(h, 3, 1))
-            g_relay_send(h, 2)
-            wait(slabs(1), g2_sem(h, 1, 0))
+        @pl.when(c == 0)
+        def _():
+            for h in range(2):
+                wait(slabs(3), g_sem.at[2 + h])
+                for d in (1, 3, 2):
+                    g_second_send(h, d)
+            for h in range(2):
+                g_forward(h, 0)
+
+    def g_lines():
+        @pl.when(c == 0)
+        def _():
+            for e in (1, 3):
+                for h in range(2):
+                    wait(slabs(4), g_sem.at[4 + h * 4 + e])
+                    g_forward(h, e)
+
+    def plane(f):
+        zz = (z + f) % 4
+        return img.at[1, zz // 2, :, :, zz % 2]
 
     def g_forward(h, e):
-        send(line(c, h, e), line(c, h, e), core_peer, S_FWD, g_sem.at[14 + h * 4 + e])
-
-    def g_forwarded(h, e):
-        wait(line(1 - c, h, e), g_sem.at[14 + h * 4 + e])
+        send(line(h, e), line(h, e), core_peer, S_FWD, g_sem.at[14 + h * 4 + e])
+
+    def p_forward(f):
+        send(plane(f), plane(f), core_peer, S_FWD, g_sem.at[14 + f])
 
     def g_last():
-        for h in range(2):
-            wait(slabs(4), g_sem.at[12 + h])
-            g_forward(h, 2)
+        @pl.when(c == 0)
+        def _():
+            for h in range(2):
+                wait(slabs(4), g_sem.at[4 + h * 4 + 2])
+                g_forward(h, 2)
+
+    def p_last():
+        @pl.when(c == 1)
+        def _():
+            for f in (1, 3, 2):
+                wait(img.at[1, 0, :, :, 0], g_sem.at[6 + (4 - f)])
+                p_forward(f)
 
     def direct_group(cc, h, e, begin=False):
         total = None
@@ -307,6 +342,20 @@
             total = term if total is None else total + term
         dacc[...] = total if begin else dacc[...] + total
 
+    def first_direct(e, begin=False):
+        @pl.when(c == 1)
+        def _():
+            for h in range(2):
+                wait(line(h, e), g_sem.at[14 + h * 4 + e])
+
+        for h in range(2):
+            direct_group(0, h, e, begin and h == 0)
+
+    def second_direct(es):
+        for h in range(2):
+            for e in es:
+                direct_group(1, h, e)
+
     def fetch(n):
         @pl.when(ga == 1)
         def _():
@@ -323,23 +372,27 @@
                 rs_dir(r, n)
 
     ld_a.wait()
-    a_wait(0)
+    for r in range(2):
+        a_wait(r, 2)
 
     @pl.when(ga == 0)
     def _():
         for n in range(CHUNKS):
             b_wait(n)
-            rs_opp(0, n)
-
-    a_wait(1)
+            for r in range(2):
+                rs_opp(r, n)
+
+    g_sum()
+
+    @pl.when(ga == 0)
+    def _():
+        for n in (2, 3):
+            b_to_ga(n)
+
+    for d in (1, 3, 0):
+        for r in range(2):
+            a_wait(r, d)
     ld_pc.start()
-
-    @pl.when(ga == 0)
-    def _():
-        for n in range(CHUNKS):
-            rs_opp(1, n)
-
-    g_sum()
 
     @pl.when(ga == 0)
     def _():
@@ -354,43 +407,36 @@
     fetch(2)
     open_late(1)
     fetch(3)
+    open_late(2)
     rs_comb(0)
-    open_late(2)
-    g_second()
     open_late(3)
     rs_comb(1)
-    g_relay_own()
     rs_comb(2)
+    g_second()
+    rs_comb(3)
     rs_second(0)
-    g_relay()
-    for h in range(2):
-        for e in (1, 3):
-            g_forward(h, e)
-    rs_comb(3)
     rs_second(1)
+    p_last()
     ld_pc.wait()
-    for h in range(2):
-        direct_group(c, h, 0, begin=h == 0)
-    for h in range(2):
-        g_forwarded(h, 0)
-        direct_group(1 - c, h, 0)
+    first_direct(0, True)
     rs_second(2)
+    g_lines()
+    rs_second(3)
+
+    @pl.when(c == 0)
+    def _():
+        for f in range(4):
+            wait(img.at[1, 0, :, :, 0], g_sem.at[14 + f])
+
+    second_direct((0, 1))
+    rs_last(0)
+    second_direct((2, 3))
+    rs_last(1)
     g_last()
-    rs_last(0)
-    for h in range(2):
-        for e in (1, 3):
-            direct_group(c, h, e)
-    rs_second(3)
-    rs_last(1)
-    for h in range(2):
-        for e in (1, 3):
-            g_forwarded(h, e)
-            direct_group(1 - c, h, e)
+    for e in (1, 3):
+        first_direct(e)
     rs_last(2)
-    for h in range(2):
-        direct_group(c, h, 2)
-        g_forwarded(h, 2)
-        direct_group(1 - c, h, 2)
+    first_direct(2)
     direct_ref[...] = dacc[...].T
     rs_last(3)
 
@@ -404,10 +450,18 @@
 
     wait(snd1, S_ONE)
     wait(snd2, S_TWO)
-    wait(img.at[0, 0, 0, pl.ds(0, 3), 0], S_Z)
-    wait(img.at[0, 0, pl.ds(0, 2), pl.ds(0, 3)], S_G1)
-    wait(img.at[0, 0], S_G2)
-    wait(img.at[0, 0, pl.ds(0, 2)], S_RELAY)
+
+    @pl.when(c == 0)
+    def _():
+        wait(img.at[0, 0, 0, pl.ds(0, 3), 0], S_Z)
+        wait(img.at[0, 0, pl.ds(0, 2), pl.ds(0, 3)], S_G1)
+        wait(img.at[0, :, pl.ds(0, 3)], S_G2)
+
+    @pl.when(c == 1)
+    def _():
+        wait(img.at[0, :, :, pl.ds(0, 3)], S_Z)
+        wait(pc_buf.at[pl.ds(0, 16), pl.ds(0, 15 * 512)], S_G1)
+
     wait(img.at[0], S_FWD)
 
 
@@ -445,8 +499,8 @@
                 pltpu.VMEM((2, CHUNKS, 7, 32, W), BF),
                 pltpu.VMEM((512, 64), F32),
                 pltpu.SemaphoreType.DMA((9,)),
-                pltpu.SemaphoreType.DMA((11,)),
-                pltpu.SemaphoreType.DMA((3, CHUNKS)),
+                pltpu.SemaphoreType.DMA((10,)),
+                pltpu.SemaphoreType.DMA((4, CHUNKS)),
                 pltpu.SemaphoreType.DMA((3, 2, CHUNKS)),
                 pltpu.SemaphoreType.DMA((22,)),
             ],

time: 41.9 us -> 38.8 us (0.926)
  Pallas kernels: 41.1 us -> 37.8 us
    pallas_call x1, Pallas kernels: 39.4 us -> 36.1 us  [local(): pl.pallas_call(kernel, out_shape=shapes, in_specs=[anywhere] * 5, out_spe...]
where the time goes in v4:
time: 38.8 us; the launch traced here: 38.4 us
  Pallas kernels  37.8 us (97%)
  between operations  0.64 us (2%)
    pallas_call x1, Pallas kernels, local(): pl.pallas_call(kernel, out_shape=shapes, in_specs=[anywhere] * 5, out_spe...  36.1 us
    pallas_call x1, Pallas kernels, local(): pl.pallas_call(write_out, out_shape=shapes)(direct, exchange)  1.68 us

profile of v4, /device:TPU:32, one launch (start us, length us, event | category | flops | bytes accessed | tf_op | source)
XLA Modules:
  0.0 38.4 jit_solution(8702279654233510774)
XLA Ops:
  0.6 36.1 %shard_map.68 = (f32[64,512]{1,0:T(8,128)}, f32[64,512]{1,0:T(8,128)}) custom-call(bf16[64,8192]{1,0:T(8,128)(2,1)} %pv_hbm.1, bf16[8192,256]{1,0:T(8,128)(2,1)} %w_hbm.1, bf16[512,16384]{1,0:T(8,128)(2,1)} %pc_hbm.1, bf16[4,2,4,2,64,256]{5,4,3,2,1,0:T(8,128)(2,1)} %bitcast.3, f32[1,256]{1,0:T(1,128)} %bitcast.4), custom_call_target="tpu_custom_call" | custom-call | flops 3221225472 | bytes 25165824 | tf_op jit(solution)/shard_map/pallas_call | solution.py:478
  36.7 1.7 %shard_map.69 = (f32[64,512]{1,0:T(8,128)}, f32[64,512]{1,0:T(8,128)}) custom-call(f32[64,512]{1,0:T(8,128)} %get-tuple-element.6.a_ref, f32[64,512]{1,0:T(8,128)} %get-tuple-element.7.b_ref), custom_call_target="tpu_custom_call" | custom-call | tf_op jit(solution)/shard_map/pallas_call | solution.py:518

commit v5 on v4

--- a/solution.py
+++ b/solution.py
@@ -206,15 +206,14 @@
             for way in range(2):
                 snd1[r, n, 2, way] = (own[way] + opp_recv[r, n, way].astype(F32)).astype(BF)
                 send(snd1.at[r, n, 2, way], near_recv.at[r, n, 2 + way], first(r, way), S_ONE, rs_sem.at[1, r, n])
-        for r in range(2):
-            acc1[r, n] = tile(r, n, ((0, 0), (0, 1)))
 
     def rs_second(n):
         for r in range(2):
+            own = tile(r, n, ((0, 0), (0, 1)))
             wait(near_recv.at[r, n], rs_sem.at[1, r, n])
             for h in range(2):
                 acc1[r, n, h] = (
-                    acc1[r, n, h] + near_recv[r, n, 1 - h].astype(F32) + near_recv[r, n, 2 + h].astype(F32)
+                    own[h] + near_recv[r, n, 1 - h].astype(F32) + near_recv[r, n, 2 + h].astype(F32)
                 )
             me = y if r == 0 else x
             for k, (e, f) in enumerate(others):
@@ -334,12 +333,12 @@
                 p_forward(f)
 
     def direct_group(cc, h, e, begin=False):
-        total = None
+        dense, images = [], []
         for j in range(4):
             xx, yy = (j, (y + e) % 4) if h == 0 else ((x + e) % 4, j)
-            cols = pl.ds(pl.multiple_of((((xx * 2 + h) * 4 + yy) * 2 + cc) * KB, KB), KB)
-            term = dot_t(pc_buf[:, cols], img[cc, h, xx, yy].reshape(64, KB))
-            total = term if total is None else total + term
+            dense.append(pc_buf[:, pl.ds(pl.multiple_of((((xx * 2 + h) * 4 + yy) * 2 + cc) * KB, KB), KB)])
+            images.append(img[cc, h, xx, yy].reshape(64, KB))
+        total = dot_t(jnp.concatenate(dense, axis=1), jnp.concatenate(images, axis=1))
         dacc[...] = total if begin else dacc[...] + total
 
     def first_direct(e, begin=False):
@@ -401,13 +400,13 @@
                 rs_dir(r, n)
 
     fetch(0)
+    open_late(0)
     fetch(1)
-    open_late(0)
     g_first()
+    open_late(1)
     fetch(2)
-    open_late(1)
+    open_late(2)
     fetch(3)
-    open_late(2)
     rs_comb(0)
     open_late(3)
     rs_comb(1)

time: 38.8 us -> 38.6 us (level)
  no operation moved by 1% of the time
where the time goes in v5:
time: 38.6 us; the launch traced here: 38.2 us
  Pallas kernels  37.5 us (97%)
  between operations  0.64 us (2%)
    pallas_call x1, Pallas kernels, local(): pl.pallas_call(kernel, out_shape=shapes, in_specs=[anywhere] * 5, out_spe...  35.8 us
    pallas_call x1, Pallas kernels, local(): pl.pallas_call(write_out, out_shape=shapes)(direct, exchange)  1.68 us

profile of v5, /device:TPU:32, one launch (start us, length us, event | category | flops | bytes accessed | tf_op | source)
XLA Modules:
  0.0 38.2 jit_solution(12738256007118498618)
XLA Ops:
  0.6 35.8 %shard_map.68 = (f32[64,512]{1,0:T(8,128)}, f32[64,512]{1,0:T(8,128)}) custom-call(bf16[64,8192]{1,0:T(8,128)(2,1)} %pv_hbm.1, bf16[8192,256]{1,0:T(8,128)(2,1)} %w_hbm.1, bf16[512,16384]{1,0:T(8,128)(2,1)} %pc_hbm.1, bf16[4,2,4,2,64,256]{5,4,3,2,1,0:T(8,128)(2,1)} %bitcast.3, f32[1,256]{1,0:T(1,128)} %bitcast.4), custom_call_target="tpu_custom_call" | custom-call | flops 3221225472 | bytes 25165824 | tf_op jit(solution)/shard_map/pallas_call | solution.py:477
  36.5 1.7 %shard_map.69 = (f32[64,512]{1,0:T(8,128)}, f32[64,512]{1,0:T(8,128)}) custom-call(f32[64,512]{1,0:T(8,128)} %get-tuple-element.6.a_ref, f32[64,512]{1,0:T(8,128)} %get-tuple-element.7.b_ref), custom_call_target="tpu_custom_call" | custom-call | tf_op jit(solution)/shard_map/pallas_call | solution.py:517
